TPU v7x, 32 devices: a whole 2x2x4 slice. The times are simulated.
32 devices in a mesh: dp: 16 (over z, x, core), tensor: 2 (over y).
Axes of the slice: x: 2, y: 2, z: 4, core: 2. Of those that a mesh axis runs over, the one named last changes fastest.
Arguments:
- inputs: bfloat16 [16384, 1024], P(('dp', 'tensor')), may hold values from -6 to 6
- qkv_weight: bfloat16 [1024, 3072], P('dp', 'tensor'), may hold values from -0.1875 to 0.1875
- qv_bias: float32 [2048], P('tensor'), may hold values from -3 to 3
- out_weight: bfloat16 [1024, 1024], P('tensor', 'dp'), may hold values from -1 to 1
- out_bias: float32 [1024], replicated, may hold values from -2 to 2
- up_weight: bfloat16 [1024, 4096], P('dp', 'tensor'), may hold values from -0.1875 to 0.1875
- up_bias: float32 [4096], P('tensor'), may hold values from -3 to 3
- down_weight: bfloat16 [4096, 1024], P('tensor', 'dp'), may hold values from -0.125 to 0.125
- down_bias: float32 [1024], replicated, may hold values from -2 to 2
- gain_one: float32 [1024], replicated, may hold values from 0.25 to 1.75
- shift_one: float32 [1024], replicated, may hold values from -2 to 2
- gain_two: float32 [1024], replicated, may hold values from 0.25 to 1.75
- shift_two: float32 [1024], replicated, may hold values from -2 to 2
- cotangent: bfloat16 [16384, 1024], P(('dp', 'tensor')), may hold values from -6 to 6
Outputs:
- layer_out: bfloat16 [16384, 1024], P(('dp', 'tensor'))
- input_grad: float32 [16384, 1024], P(('dp', 'tensor'))
- qkv_weight_grad: float32 [1024, 3072], P('dp', 'tensor')
- qv_bias_grad: float32 [2048], P('tensor')
- out_weight_grad: float32 [1024, 1024], P('tensor', 'dp')
- out_bias_grad: float32 [1024], replicated
- up_weight_grad: float32 [1024, 4096], P('dp', 'tensor')
- up_bias_grad: float32 [4096], P('tensor')
- down_weight_grad: float32 [4096, 1024], P('tensor', 'dp')
- down_bias_grad: float32 [1024], replicated
- gain_one_grad: float32 [1024], replicated
- shift_one_grad: float32 [1024], replicated
- gain_two_grad: float32 [1024], replicated
- shift_two_grad: float32 [1024], replicated
All inputs are finite; a program needn't handle non-finite values.
Results may differ from a plain program's by a relative error of at most 0.015.
Values may be sent and summed in bfloat16 or wider, within the bound.
A program may use at most 192 MiB of HBM per device.

v0:
```python
import math

import jax
import jax.numpy as jnp
from jax import lax
from jax.sharding import PartitionSpec as P

HD = 64
LEN = 1024


eps = 1e-05


def normalize(values_in, gain_vec, shift_vec):
    row_mean = jnp.mean(values_in, axis=-1, keepdims=True)
    centred = values_in - row_mean
    row_var = jnp.mean(centred * centred, axis=-1, keepdims=True)
    return centred * lax.rsqrt(row_var + eps) * gain_vec + shift_vec


def gelu_tanh(hidden):
    return jax.nn.gelu(hidden, approximate=True)


def contract_rows(left, right):
    return lax.dot_general(
        left, right, (((0,), (0,)), ((), ())), preferred_element_type=jnp.float32
    )


def contract_cols(left, right):
    return lax.dot_general(
        left, right, (((1,), (1,)), ((), ())), preferred_element_type=jnp.float32
    )


def rows_all(local_rows):
    return lax.all_gather(local_rows, "tensor", axis=0, tiled=True)


def rows_sum(left, right, transposed):

    def term():
        if transposed:
            return contract_cols(left, right)
        return jnp.dot(left, right, preferred_element_type=jnp.float32)

    return lax.psum_scatter(term(), "tensor", scatter_dimension=0, tiled=True)


def causal_mask(block_idx, block_rows, length):
    row_ids = block_idx * block_rows + jnp.arange(block_rows)
    return jnp.arange(length)[None, :] <= row_ids[:, None]


def attend_forward(queries, key_rows, value_rows):
    length = queries.shape[0]
    block_rows = min(512, length)
    block_count = length // block_rows
    score_scale = 1.0 / math.sqrt(queries.shape[-1])
    query_blocks = queries.reshape(block_count, block_rows, queries.shape[1], queries.shape[2])

    def block_attend(pair_in):
        query_block, block_idx = pair_in
        scores = (
            jnp.einsum("qhe,khe->hqk", query_block, key_rows, preferred_element_type=jnp.float32)
            * score_scale
        )
        allowed = causal_mask(block_idx, block_rows, length)
        scores = jnp.where(allowed[None], scores, -1e30)
        row_peak = jnp.max(scores, axis=-1, keepdims=True)
        exp_scores = jnp.exp(scores - row_peak)
        row_total = jnp.sum(exp_scores, axis=-1, keepdims=True)
        probs_low = (exp_scores / row_total).astype(jnp.bfloat16)
        outputs = jnp.einsum(
            "hqk,khe->qhe", probs_low, value_rows, preferred_element_type=jnp.float32
        )
        log_total = (row_peak + jnp.log(row_total))[..., 0]
        return (outputs, log_total)

    outputs, log_total = lax.map(block_attend, (query_blocks, jnp.arange(block_count)))
    return (outputs.reshape(queries.shape), log_total)


def attend_backward(queries, key_rows, value_rows, heads_grad, log_total):
    length = queries.shape[0]
    block_rows = min(512, length)
    block_count = length // block_rows
    score_scale = 1.0 / math.sqrt(queries.shape[-1])
    block_shape = (block_count, block_rows, queries.shape[1], queries.shape[2])

    def block_back(carry, pair_in):
        key_grad, value_grad = carry
        query_block, grad_block, lse_block, block_idx = pair_in
        scores = (
            jnp.einsum("qhe,khe->hqk", query_block, key_rows, preferred_element_type=jnp.float32)
            * score_scale
        )
        allowed = causal_mask(block_idx, block_rows, length)
        probs = jnp.where(allowed[None], jnp.exp(scores - lse_block[..., None]), 0.0)
        prob_grad = jnp.einsum(
            "qhe,khe->hqk", grad_block, value_rows, preferred_element_type=jnp.float32
        )
        row_dot = jnp.sum(probs * prob_grad, axis=-1, keepdims=True)
        score_grad = (probs * (prob_grad - row_dot)).astype(jnp.bfloat16)
        query_grad = (
            jnp.einsum("hqk,khe->qhe", score_grad, key_rows, preferred_element_type=jnp.float32)
            * score_scale
        )
        key_grad = (
            key_grad
            + jnp.einsum(
                "hqk,qhe->khe", score_grad, query_block, preferred_element_type=jnp.float32
            )
            * score_scale
        )
        value_grad = value_grad + jnp.einsum(
            "hqk,qhe->khe",
            probs.astype(jnp.bfloat16),
            grad_block,
            preferred_element_type=jnp.float32,
        )
        return ((key_grad, value_grad), query_grad)

    zero_rows = jnp.zeros(queries.shape, jnp.float32)
    (key_grad, value_grad), query_grad = lax.scan(
        block_back,
        (zero_rows, zero_rows),
        (
            queries.reshape(block_shape),
            heads_grad.reshape(block_shape),
            log_total,
            jnp.arange(block_count),
        ),
    )
    return (query_grad.reshape(queries.shape), key_grad, value_grad)


def shards(
    inputs,
    qkv_weight,
    qv_bias,
    out_weight,
    out_bias,
    up_weight,
    up_bias,
    down_weight,
    down_bias,
    gain_one,
    shift_one,
    gain_two,
    shift_two,
    cotangent,
):
    local_x = inputs.astype(jnp.float32)
    qkv_full, out_full, up_full, down_full = (
        lax.all_gather(qkv_weight, "dp", axis=0, tiled=True),
        lax.all_gather(out_weight, "dp", axis=1, tiled=True),
        lax.all_gather(up_weight, "dp", axis=0, tiled=True),
        lax.all_gather(down_weight, "dp", axis=1, tiled=True),
    )
    first_norm = normalize(local_x, gain_one, shift_one)
    normed_all = rows_all(first_norm.astype(jnp.bfloat16))
    group_rows = normed_all.shape[0]
    head_count = qv_bias.shape[0] // (2 * HD)
    seq_count = group_rows // LEN
    mixed_qkv = jnp.dot(normed_all, qkv_full, preferred_element_type=jnp.float32).reshape(
        group_rows, head_count, 3, HD
    )
    biases = qv_bias.reshape(head_count, 2, HD)
    queries = (mixed_qkv[:, :, 0] + biases[:, 0]).astype(jnp.bfloat16)
    key_rows = mixed_qkv[:, :, 1].astype(jnp.bfloat16)
    value_rows = (mixed_qkv[:, :, 2] + biases[:, 1]).astype(jnp.bfloat16)

    def split_seq(array_in):
        return array_in.reshape(seq_count, LEN, head_count, HD)

    def forward_seq(triple_in):
        return attend_forward(triple_in[0], triple_in[1], triple_in[2])

    heads_out, log_total = lax.map(
        forward_seq, (split_seq(queries), split_seq(key_rows), split_seq(value_rows))
    )
    heads_low = heads_out.reshape(group_rows, head_count * HD).astype(jnp.bfloat16)
    branch = rows_sum(heads_low, out_full, False) + out_bias
    middle = local_x + branch
    second_norm = normalize(middle, gain_two, shift_two)
    second_all = rows_all(second_norm.astype(jnp.bfloat16))
    hidden = jnp.dot(second_all, up_full, preferred_element_type=jnp.float32) + up_bias
    active_low = gelu_tanh(hidden).astype(jnp.bfloat16)
    down_out = rows_sum(active_low, down_full, False) + down_bias
    layer_out = (middle + down_out).astype(jnp.bfloat16)
    back_qkv, back_out, back_up, back_down = (
        lax.all_gather(qkv_weight, "dp", axis=0, tiled=True),
        lax.all_gather(out_weight, "dp", axis=1, tiled=True),
        lax.all_gather(up_weight, "dp", axis=0, tiled=True),
        lax.all_gather(down_weight, "dp", axis=1, tiled=True),
    )
    out_grad = cotangent.astype(jnp.float32)
    down_bias_grad = jnp.sum(out_grad, axis=0)
    down_all = rows_all(cotangent)
    down_weight_grad = contract_rows(active_low, down_all)
    active_grad = contract_cols(down_all, back_down)
    gelu_value, gelu_pull = jax.vjp(gelu_tanh, hidden)
    hidden_low = gelu_pull(active_grad)[0].astype(jnp.bfloat16)
    up_bias_grad = jnp.sum(hidden_low, axis=0, dtype=jnp.float32)
    up_weight_grad = contract_rows(second_all, hidden_low)
    second_grad = rows_sum(hidden_low, back_up, True)
    norm_value, norm_pull = jax.vjp(normalize, middle, gain_two, shift_two)
    middle_part, gain_two_grad, shift_two_grad = norm_pull(second_grad)
    middle_grad = out_grad + middle_part
    branch_low = middle_grad.astype(jnp.bfloat16)
    out_bias_grad = jnp.sum(branch_low, axis=0, dtype=jnp.float32)
    branch_all = rows_all(branch_low)
    out_weight_grad = contract_rows(heads_low, branch_all)
    heads_grad = contract_cols(branch_all, back_out).astype(jnp.bfloat16)

    def backward_seq(group_in):
        return attend_backward(group_in[0], group_in[1], group_in[2], group_in[3], group_in[4])

    query_grad, key_grad, value_grad = lax.map(
        backward_seq,
        (
            split_seq(queries),
            split_seq(key_rows),
            split_seq(value_rows),
            split_seq(heads_grad),
            log_total,
        ),
    )
    stacked = (
        jnp.stack((query_grad, key_grad, value_grad), axis=3)
        .reshape(group_rows, head_count, 3, HD)
        .astype(jnp.bfloat16)
    )
    bias_sums = jnp.sum(stacked, axis=0, dtype=jnp.float32)
    qv_bias_grad = jnp.stack((bias_sums[:, 0], bias_sums[:, 2]), axis=1).reshape(-1)
    qkv_low = stacked.reshape(group_rows, head_count * 3 * HD)
    qkv_weight_grad = contract_rows(normed_all, qkv_low)
    first_grad = rows_sum(qkv_low, back_qkv, True)
    first_value, first_pull = jax.vjp(normalize, local_x, gain_one, shift_one)
    input_part, gain_one_grad, shift_one_grad = first_pull(first_grad)
    input_grad = middle_grad + input_part
    qkv_shard, out_shard, up_shard, down_shard = (
        lax.psum_scatter(
            qkv_weight_grad.astype(jnp.bfloat16), "dp", scatter_dimension=0, tiled=True
        ).astype(jnp.float32),
        lax.psum_scatter(
            out_weight_grad.astype(jnp.bfloat16), "dp", scatter_dimension=1, tiled=True
        ).astype(jnp.float32),
        lax.psum_scatter(
            up_weight_grad.astype(jnp.bfloat16), "dp", scatter_dimension=0, tiled=True
        ).astype(jnp.float32),
        lax.psum_scatter(
            down_weight_grad.astype(jnp.bfloat16), "dp", scatter_dimension=1, tiled=True
        ).astype(jnp.float32),
    )
    (
        out_bias_total,
        down_bias_total,
        gain_one_total,
        shift_one_total,
        gain_two_total,
        shift_two_total,
    ) = lax.psum(
        (
            out_bias_grad,
            down_bias_grad,
            gain_one_grad,
            shift_one_grad,
            gain_two_grad,
            shift_two_grad,
        ),
        ("dp", "tensor"),
    )
    qv_bias_total, up_bias_total = lax.psum((qv_bias_grad, up_bias_grad), "dp")
    return (
        layer_out,
        input_grad,
        qkv_shard,
        qv_bias_total,
        out_shard,
        out_bias_total,
        up_shard,
        up_bias_total,
        down_shard,
        down_bias_total,
        gain_one_total,
        shift_one_total,
        gain_two_total,
        shift_two_total,
    )


def solution(mesh):
    in_specs = (
        P(("dp", "tensor"), None),
        P("dp", "tensor"),
        P("tensor"),
        P("tensor", "dp"),
        P(),
        P("dp", "tensor"),
        P("tensor"),
        P("tensor", "dp"),
        P(),
        P(),
        P(),
        P(),
        P(),
        P(("dp", "tensor"), None),
    )
    out_specs = (
        P(("dp", "tensor"), None),
        P(("dp", "tensor"), None),
        P("dp", "tensor"),
        P("tensor"),
        P("tensor", "dp"),
        P(),
        P("dp", "tensor"),
        P("tensor"),
        P("tensor", "dp"),
        P(),
        P(),
        P(),
        P(),
        P(),
    )
    return jax.shard_map(shards, mesh=mesh, in_specs=in_specs, out_specs=out_specs, check_vma=False)
```

profile of v0, /device:TPU:0, one launch (start us, length us, event | category | flops | bytes accessed | tf_op | source)
XLA Modules:
  0.0 937.5 jit_solution(10040735607031805842)
XLA Ops:
  14.7 34.3 %all-gather.9.cloned.1.call-done = bf16[1024,1024]{1,0:T(8,128)(2,1)} async-done(((bf16[512,1024]{1,0:T(8,128)(2,1)}), bf16[1024,1024]{1,0:T(8,128)(2,1)}) %all-gather.9.cloned.1.call-update) | async-done | bytes 2097168 | tf_op jit(solution)/shard_map/all_gather | solution.py:39
  49.0 47.5 %all-gather.11.cloned.1.call-done = bf16[1024,1536]{1,0:T(8,128)(2,1)} async-done(((bf16[64,1536]{1,0:T(8,128)(2,1)}), bf16[1024,1536]{1,0:T(8,128)(2,1)}) %all-gather.11.cloned.1.call-update) | async-done | bytes 3145744 | tf_op jit(solution)/shard_map/all_gather | solution.py:158
  96.5 6.2 fusion.62
  110.7 31.9 %while.47 = (s32[]{:T(128)}, bf16[2,512,8,64]{1,3,2,0:T(8,128)(2,1)S(1)}, f32[2,8,512]{2,1,0:T(8,128)S(1)}, s32[2]{0:T(128)S(1)}, bf16[2,512,8,64]{1,3,2,0:T(8,1...) while((s32[]{:T(128)}, ...), condition=%wide.region_5.6_spmd, body=%wide.region_2.5_spmd.sunk | while | flops 1124594176 | bytes 56234124 | solution.py:82
  149.9 52.1 %reduce-scatter.9.cloned.1.call-done = f32[512,1024]{1,0:T(8,128)} async-done(((f32[1024,1024]{1,0:T(8,128)}), f32[512,1024]{1,0:T(8,128)}) %reduce-scatter.9.cloned.1.call-update) | async-done | bytes 2097168 | tf_op jit(solution)/shard_map/reduce_scatter | solution.py:49
  207.6 47.3 %all-gather.17.cloned.1.call-done = bf16[1024,2048]{1,0:T(8,128)(2,1)} async-done(((bf16[64,2048]{1,0:T(8,128)(2,1)}), bf16[1024,2048]{1,0:T(8,128)(2,1)}) %all-gather.17.cloned.1.call-update) | async-done | bytes 4194320 | tf_op jit(solution)/shard_map/all_gather | solution.py:160
  254.9 33.7 %all-gather.15.cloned.1.call-done = bf16[1024,1024]{1,0:T(8,128)(2,1)} async-done(((bf16[512,1024]{1,0:T(8,128)(2,1)}), bf16[1024,1024]{1,0:T(8,128)(2,1)}) %all-gather.15.cloned.1.call-update) | async-done | bytes 2097168 | tf_op jit(solution)/shard_map/all_gather | solution.py:39
  288.6 10.9 %fusion.64 = f32[1024,2048]{1,0:T(8,128)} fusion(bf16[1024,1024]{1,0:T(8,128)(2,1)} %all-gather.15.cloned.1.call-done, bf16[1024,2048]{1,0:T(8,128)(2,1)} %all-gather.17.cloned.1.call-done), kind=kOutput, calls=%fused_computation.112 | convolution fusion | flops 4294967296 | bytes 14680064 | tf_op jit(solution)/shard_map/dot_general | solution.py:190
  299.4 23.9 %all-gather.21.cloned.1.call-done = bf16[1024,1024]{1,0:T(8,128)(2,1)} async-done(((bf16[512,1024]{1,0:T(8,128)(2,1)}), bf16[1024,1024]{1,0:T(8,128)(2,1)}) %all-gather.21.cloned.1.call-update) | async-done | bytes 2097168 | tf_op jit(solution)/shard_map/all_gather | solution.py:39
  323.3 53.0 %all-gather.19.cloned.1.call-done = bf16[2048,1024]{0,1:T(8,128)(2,1)} async-done(((bf16[2048,64]{0,1:T(8,128)(2,1)}), bf16[2048,1024]{0,1:T(8,128)(2,1)}) %all-gather.19.cloned.1.call-update) | async-done | bytes 4194320 | tf_op jit(solution)/shard_map/all_gather | solution.py:161
  376.3 13.7 %convert_reduce_fusion = (f32[2048]{0:T(1024)}, bf16[1024,2048]{1,0:T(8,128)(2,1)S(1)}) fusion(f32[1024,2048]{1,0:T(8,128)} %fusion.64, f32[2048]{0:T(1024)S(1)} %copy-done.39, bf16[1024,1024]{1,0:T(8,128)(2,1)} %all-gather.21.cloned.1.call-done, bf16[2048,1024]{0,1:T(8,128)(2,1)} %all-gather.19.cloned.1.call-done), kind=kOutput, calls=%fused_computation.51 | convolution fusion | flops 4343199744 | bytes 18890752 | tf_op jit(solution)/shard_map/dot_general | solution.py:33
  392.0 6.1 fusion.65
  398.3 12.1 %fusion.54 = f32[1024,1024]{1,0:T(8,128)} fusion(bf16[2048,1024]{0,1:T(8,128)(2,1)} %all-gather.19.cloned.1.call-done, f32[1024,2048]{1,0:T(8,128)} %fusion.64, f32[2048]{0:T(1024)S(1)} %copy-done.39), kind=kOutput, calls=%fused_computation.104 | convolution fusion | flops 4315938816 | bytes 16785408 | tf_op jit(solution)/shard_map/dot_general | solution.py:47
  410.5 40.6 %reduce-scatter.13.cloned.1.call-done = f32[512,1024]{1,0:T(8,128)} async-done(((f32[1024,1024]{1,0:T(8,128)}), f32[512,1024]{1,0:T(8,128)}) %reduce-scatter.13.cloned.1.call-update) | async-done | bytes 2097168 | tf_op jit(solution)/shard_map/reduce_scatter | solution.py:49
  454.0 53.5 %reduce-scatter.11.cloned.1.call-done = f32[512,1024]{1,0:T(8,128)} async-done(((f32[1024,1024]{1,0:T(8,128)}), f32[512,1024]{1,0:T(8,128)}) %reduce-scatter.11.cloned.1.call-update) | async-done | bytes 2097168 | tf_op jit(solution)/shard_map/reduce_scatter | solution.py:49
  515.0 10.4 %convolution_convert_fusion.1 = bf16[2048,1024]{0,1:T(8,128)(2,1)} fusion(bf16[1024,1024]{1,0:T(8,128)(2,1)S(1)} %copy-done.37, f32[1024,2048]{1,0:T(8,128)} %fusion.64, f32[2048]{0:T(1024)S(1)} %copy-done.39), kind=kOutput, calls=%fused_computation.56 | convolution fusion | flops 4318035968 | bytes 14688256 | tf_op jit(solution)/shard_map/dot_general | solution.py:27
  527.0 8.3 convolution_convert_fusion.2
  535.4 12.8 %all-gather.23.cloned.1.call-done = bf16[1024,1024]{1,0:T(8,128)(2,1)} async-done(((bf16[512,1024]{1,0:T(8,128)(2,1)}), bf16[1024,1024]{1,0:T(8,128)(2,1)}) %all-gather.23.cloned.1.call-update) | async-done | bytes 2097168 | tf_op jit(solution)/shard_map/all_gather | solution.py:39
  561.9 126.8 %while.48 = (s32[]{:T(128)}, f32[1024,8,64]{0,2,1:T(8,128)}, f32[1024,8,64]{0,2,1:T(8,128)}, bf16[2,512,8,64]{1,0,3,2:T(2,128)(2,1)}, bf16[2,512,8,64]{1,3,2,0:T...) while((s32[]{:T(128)}, f32[1024,8,64]{0,2,1:T(8,128)}, ...), condition=%wide.region_15.16_spmd.clone, body=%wide.region_13.15_spmd.clone.sunk | while | flops 2725769728 | bytes 198005104 | solution.py:127
  568.8 11.3 %multiply_reduce_fusion.5 = (f32[8,512]{1,0:T(8,128)}, f32[8,512,1024]{2,1,0:T(8,128)}) fusion(f32[8,512,1024]{2,1,0:T(8,128)S(1)} %fusion.126, f32[8,512]{1,0:T(8,128)} %dynamic-slice_bitcast_fusion.2, bf16[1024,8,64]{0,2,1:T(8,128)(2,1)S(1)} %get-tuple-element.491, bf16[2,512,8,64]{1,3,2,0:T(8,128)(2,1)} %get-tuple-element.489, s32[]{:T(128)S(6)} %copy.96, ...), kind=kOutput, calls=%fused_computation.18.clone.1 | convolution fusion | flops 557838336 | bytes 35684356 | tf_op jit(solution)/shard_map/while/body/eval_jaxpr/while/body/eval_jaxpr/qhe,khe->hqk/dot_general | solution.py:97
  580.1 9.8 %multiply_convert_fusion.5 = bf16[8,512,1024]{2,1,0:T(8,128)(2,1)} fusion(f32[8,512,1024]{2,1,0:T(8,128)} %get-tuple-element.430, f32[8,512,1024]{2,1,0:T(8,128)S(1)} %fusion.126, f32[8,512]{1,0:T(8,128)} %get-tuple-element.431), kind=kLoop, calls=%fused_computation.17.clone.1 | loop fusion | flops 12582912 | bytes 41959424 | tf_op jit(solution)/shard_map/while/body/eval_jaxpr/while/body/eval_jaxpr/convert_element_type | solution.py:106
  589.9 8.9 bitcast_add_fusion.5
  606.2 18.6 %dynamic_update_slice.31 = bf16[2,512,8,64]{1,0,3,2:T(2,128)(2,1)} dynamic-update-slice(bf16[2,512,8,64]{1,0,3,2:T(2,128)(2,1)} %get-tuple-element.475, bf16[1,512,8,64]{1,0,3,2:T(2,128)(2,1)} %copy.79, s32[]{:T(128)S(6)} %copy.96, s32[]{:T(128)} %constant.95.clone.1..sunk, s32[]{:T(128)} %constant.95.clone.1..sunk, s32[]{:T(128)} %constant.95.clone.1..sunk) | dynamic-update-slice | bytes 1048580 | tf_op jit(solution)/shard_map/while/body/eval_jaxpr/while/body/jit(dynamic_update_index_in_dim)/dynamic_update_slice | solution.py:82
  631.6 11.3 %multiply_reduce_fusion.5 = (f32[8,512]{1,0:T(8,128)}, f32[8,512,1024]{2,1,0:T(8,128)}) fusion(f32[8,512,1024]{2,1,0:T(8,128)S(1)} %fusion.126, f32[8,512]{1,0:T(8,128)} %dynamic-slice_bitcast_fusion.2, bf16[1024,8,64]{0,2,1:T(8,128)(2,1)S(1)} %get-tuple-element.491, bf16[2,512,8,64]{1,3,2,0:T(8,128)(2,1)} %get-tuple-element.489, s32[]{:T(128)S(6)} %copy.96, ...), kind=kOutput, calls=%fused_computation.18.clone.1 | convolution fusion | flops 557838336 | bytes 35684356 | tf_op jit(solution)/shard_map/while/body/eval_jaxpr/while/body/eval_jaxpr/qhe,khe->hqk/dot_general | solution.py:97
  642.9 9.8 %multiply_convert_fusion.5 = bf16[8,512,1024]{2,1,0:T(8,128)(2,1)} fusion(f32[8,512,1024]{2,1,0:T(8,128)} %get-tuple-element.430, f32[8,512,1024]{2,1,0:T(8,128)S(1)} %fusion.126, f32[8,512]{1,0:T(8,128)} %get-tuple-element.431), kind=kLoop, calls=%fused_computation.17.clone.1 | loop fusion | flops 12582912 | bytes 41959424 | tf_op jit(solution)/shard_map/while/body/eval_jaxpr/while/body/eval_jaxpr/convert_element_type | solution.py:106
  652.7 10.0 %bitcast_add_fusion.5 = f32[1024,8,64]{0,2,1:T(8,128)} fusion(f32[1024,8,64]{0,2,1:T(8,128)} %get-tuple-element.474, f32[8,512,1024]{2,1,0:T(8,128)} %get-tuple-element.430, pred[]{:T(512)S(6)} %compare.3, bf16[2,512,8,64]{1,3,2,0:T(8,128)(2,1)S(1)} %copy-done.5, s32[]{:T(128)S(6)} %copy.96), kind=kOutput, calls=%fused_computation.22.clone.1 | convolution fusion | flops 542113792 | bytes 21495812 | tf_op jit(solution)/shard_map/while/body/eval_jaxpr/while/body/eval_jaxpr/hqk,qhe->khe/dot_general | solution.py:118
  670.1 18.6 %dynamic_update_slice.31 = bf16[2,512,8,64]{1,0,3,2:T(2,128)(2,1)} dynamic-update-slice(bf16[2,512,8,64]{1,0,3,2:T(2,128)(2,1)} %get-tuple-element.475, bf16[1,512,8,64]{1,0,3,2:T(2,128)(2,1)} %copy.79, s32[]{:T(128)S(6)} %copy.96, s32[]{:T(128)} %constant.95.clone.1..sunk, s32[]{:T(128)} %constant.95.clone.1..sunk, s32[]{:T(128)} %constant.95.clone.1..sunk) | dynamic-update-slice | bytes 1048580 | tf_op jit(solution)/shard_map/while/body/eval_jaxpr/while/body/jit(dynamic_update_index_in_dim)/dynamic_update_slice | solution.py:82
  699.9 8.4 fusion.66
  712.2 62.6 %all-reduce.1 = (f32[1024]{0:T(1024)}, f32[2048]{0:T(1024)}) all-reduce(f32[1024]{0:T(1024)S(1)} %reshape.231, f32[2048]{0:T(1024)S(1)} %copy-done.29), channel_id=1, replica_groups=mesh['dp'=16,'tensor'=2] {'dp'}, use_global_device_ids=true, to_apply=%region_21.22 | all-reduce | flops 3072 | bytes 24576 | tf_op jit(solution)/shard_map/psum | solution.py:277
  776.3 53.5 %reduce-scatter.17.cloned.1.call-done = bf16[64,1536]{1,0:T(8,128)(2,1)} async-done(((bf16[1024,1536]{1,0:T(8,128)(2,1)}), bf16[64,1536]{1,0:T(8,128)(2,1)}) %reduce-scatter.17.cloned.1.call-update) | async-done | bytes 196624 | tf_op jit(solution)/shard_map/reduce_scatter | solution.py:246
  831.5 53.7 %reduce-scatter.15.cloned.1.call-done = f32[512,1024]{1,0:T(8,128)} async-done(((f32[1024,1024]{1,0:T(8,128)}), f32[512,1024]{1,0:T(8,128)}) %reduce-scatter.15.cloned.1.call-update) | async-done | bytes 2097168 | tf_op jit(solution)/shard_map/reduce_scatter | solution.py:49
  890.8 40.0 %all-reduce = (f32[1024]{0:T(1024)}, f32[1024]{0:T(1024)}, f32[1024]{0:T(1024)}, f32[1024]{0:T(1024)}, f32[1024]{0:T(1024)}, /*index=5*/f32[1024]{0:T(1024)}) all-reduce(f32[1024]{0:T(1024)S(1)} %copy-done.26, f32[1024]{0:T(1024)S(1)} %get-tuple-element.314, ...), channel_id=1, replica_groups=mesh['dp'=16,'tensor'=2] {'dp','tensor'}, use_global_device_ids=true, to_apply=%region_24.25 | all-reduce | flops 6144 | bytes 49152 | tf_op jit(solution)/shard_map/psum | solution.py:266
  (214 shorter events, 137.3 us)
Async XLA Ops:
  7.2 41.8 %all-gather.9.cloned.1.call-start = ((), (), s32[]{:S(2)}) async-start(), calls=%async_computation.8 | async-start | bytes 3145728 | tf_op jit(solution)/shard_map/all_gather | solution.py:39
  8.7 94.0 %copy-start.16 = (f32[512]{0:T(512)}, f32[512]{0:T(512)S(1)}, u32[]{:S(2)}) copy-start(f32[512]{0:T(512)S(1)} %broadcast_multiply_fusion.1) | copy-start | bytes 6148
  13.0 83.5 %all-gather.11.cloned.1.call-start = ((), (), s32[]{:S(2)}) async-start(), calls=%async_computation.9 | async-start | bytes 3342336 | tf_op jit(solution)/shard_map/all_gather | solution.py:158
  13.8 130.2 %all-gather.13.cloned.1.call-start = ((), (), s32[]{:S(2)}) async-start(), calls=%async_computation.10 | async-start | bytes 1114112 | tf_op jit(solution)/shard_map/all_gather | solution.py:159
  14.5 187.5 %reduce-scatter.9.cloned.1.call-start = ((), (), s32[]{:S(2)}) async-start(), calls=%async_computation.11 | async-start | bytes 6291456 | tf_op jit(solution)/shard_map/reduce_scatter | solution.py:49
  148.9 53.2 %copy-start.33 = (f32[1024]{0:T(1024)S(1)}, f32[1024]{0:T(1024)}, u32[]{:S(2)}) copy-start(f32[1024]{0:T(1024)} %param.22) | copy-start | bytes 12292
  148.9 106.0 %all-gather.17.cloned.1.call-start = ((), (), s32[]{:S(2)}) async-start(), calls=%async_computation.13 | async-start | bytes 4456448 | tf_op jit(solution)/shard_map/all_gather | solution.py:160
  149.5 55.1 %copy-start.19 = (f32[1024]{0:T(1024)S(1)}, f32[1024]{0:T(1024)}, u32[]{:S(2)}) copy-start(f32[1024]{0:T(1024)} %param.29) | copy-start | bytes 12292
  149.5 55.1 %copy-start.30 = (f32[1024]{0:T(1024)S(1)}, f32[1024]{0:T(1024)}, u32[]{:S(2)}) copy-start(f32[1024]{0:T(1024)} %param.30) | copy-start | bytes 12292
  149.5 139.1 %all-gather.15.cloned.1.call-start = ((), (), s32[]{:S(2)}) async-start(), calls=%async_computation.12 | async-start | bytes 3145728 | tf_op jit(solution)/shard_map/all_gather | solution.py:39
  206.0 117.3 %all-gather.21.cloned.1.call-start = ((), (), s32[]{:S(2)}) async-start(), calls=%async_computation.16 | async-start | bytes 3145728 | tf_op jit(solution)/shard_map/all_gather | solution.py:39
  206.8 169.5 %all-gather.19.cloned.1.call-start = ((), (), s32[]{:S(2)}) async-start(), calls=%async_computation.14 | async-start | bytes 4456448 | tf_op jit(solution)/shard_map/all_gather | solution.py:161
  207.5 168.8 %copy-start.39 = (f32[2048]{0:T(1024)S(1)}, f32[2048]{0:T(1024)}, u32[]{:S(2)}) copy-start(f32[2048]{0:T(1024)} %param.24) | copy-start | bytes 24580
  207.5 243.5 %reduce-scatter.13.cloned.1.call-start = ((), (), s32[]{:S(2)}) async-start(), calls=%async_computation.17 | async-start | bytes 6291456 | tf_op jit(solution)/shard_map/reduce_scatter | solution.py:49
  398.1 109.4 %reduce-scatter.11.cloned.1.call-start = ((), (), s32[]{:S(2)}) async-start(), calls=%async_computation.15 | async-start | bytes 6291456 | tf_op jit(solution)/shard_map/reduce_scatter | solution.py:49
  410.5 97.1 %copy-start.31 = (f32[1024]{0:T(1024)S(1)}, f32[1024]{0:T(1024)}, u32[]{:S(2)}) copy-start(f32[1024]{0:T(1024)} %param.26) | copy-start | bytes 12292
  410.5 137.8 %all-gather.23.cloned.1.call-start = ((), (), s32[]{:S(2)}) async-start(), calls=%async_computation.18 | async-start | bytes 3145728 | tf_op jit(solution)/shard_map/all_gather | solution.py:39
  514.9 193.5 %reduce-scatter.23.cloned.1.call-start = ((), (), s32[]{:S(2)}) async-start(), calls=%async_computation.23 | async-start | bytes 4456448 | tf_op jit(solution)/shard_map/reduce_scatter | solution.py:255
  525.4 184.9 %reduce-scatter.21.cloned.1.call-start = ((), (), s32[]{:S(2)}) async-start(), calls=%async_computation.22 | async-start | bytes 4456448 | tf_op jit(solution)/shard_map/reduce_scatter | solution.py:252
  535.3 239.5 %reduce-scatter.19.cloned.1.call-start = ((), (), s32[]{:S(2)}) async-start(), calls=%async_computation.21 | async-start | bytes 1114112 | tf_op jit(solution)/shard_map/reduce_scatter | solution.py:249
  561.4 268.4 %reduce-scatter.17.cloned.1.call-start = ((), (), s32[]{:S(2)}) async-start(), calls=%async_computation.20 | async-start | bytes 3342336 | tf_op jit(solution)/shard_map/reduce_scatter | solution.py:246
  604.3 20.5 %copy-start.2 = (f32[1024,8,64]{0,2,1:T(8,128)}, f32[1024,8,64]{0,2,1:T(8,128)S(1)}, u32[]{:S(2)}) copy-start(f32[1024,8,64]{0,2,1:T(8,128)S(1)} %bitcast_add_fusion.4) | copy-start | bytes 6291460 | tf_op jit(solution)/shard_map/while/body/eval_jaxpr/while
  668.2 20.5 %copy-start.2 = (f32[1024,8,64]{0,2,1:T(8,128)}, f32[1024,8,64]{0,2,1:T(8,128)S(1)}, u32[]{:S(2)}) copy-start(f32[1024,8,64]{0,2,1:T(8,128)S(1)} %bitcast_add_fusion.4) | copy-start | bytes 6291460 | tf_op jit(solution)/shard_map/while/body/eval_jaxpr/while
  668.2 20.5 %copy-start.15 = (f32[2,8,512]{2,1,0:T(8,128)S(1)}, f32[2,8,512]{2,1,0:T(8,128)}, u32[]{:S(2)}) copy-start(f32[2,8,512]{2,1,0:T(8,128)} %copy-done.14) | copy-start | bytes 98308 | tf_op jit(solution)/shard_map/while/body/eval_jaxpr/while
  699.9 185.3 %reduce-scatter.15.cloned.1.call-start = ((), (), s32[]{:S(2)}) async-start(), calls=%async_computation.19 | async-start | bytes 6291456 | tf_op jit(solution)/shard_map/reduce_scatter | solution.py:49
  708.3 176.8 %copy-start.4 = (bf16[512,1024]{1,0:T(8,128)(2,1)S(1)}, bf16[512,1024]{1,0:T(8,128)(2,1)}, u32[]{:S(2)}) copy-start(bf16[512,1024]{1,0:T(8,128)(2,1)} %param.18) | copy-start | bytes 3145732
  708.3 176.8 %copy-start.17 = (f32[512]{0:T(512)S(1)}, f32[512]{0:T(512)}, u32[]{:S(2)}) copy-start(f32[512]{0:T(512)} %copy-done.16) | copy-start | bytes 6148
  708.3 176.8 %copy-start.18 = (f32[1024]{0:T(1024)S(1)}, f32[1024]{0:T(1024)}, u32[]{:S(2)}) copy-start(f32[1024]{0:T(1024)} %param.27) | copy-start | bytes 12292
  708.4 179.1 %copy-start.25 = (f32[512]{0:T(512)S(1)}, f32[512]{0:T(512)}, u32[]{:S(2)}) copy-start(f32[512]{0:T(512)} %copy-done.24) | copy-start | bytes 6148
  708.4 179.1 %copy-start.21 = (f32[512]{0:T(512)S(1)}, f32[512]{0:T(512)}, u32[]{:S(2)}) copy-start(f32[512]{0:T(512)} %copy-done.20) | copy-start | bytes 6148
  831.5 57.0 %copy-start.10 = (bf16[512,1024]{1,0:T(8,128)(2,1)S(1)}, bf16[512,1024]{1,0:T(8,128)(2,1)}, u32[]{:S(2)}) copy-start(bf16[512,1024]{1,0:T(8,128)(2,1)} %param.31) | copy-start | bytes 3145732
  831.5 57.0 %copy-start.23 = (f32[512]{0:T(512)S(1)}, f32[512]{0:T(512)}, u32[]{:S(2)}) copy-start(f32[512]{0:T(512)} %copy-done.22) | copy-start | bytes 6148
  (31 other events, 160.0 us)
Sparse Core Ops, SparseCore 0:
  13.2 35.8 all-gather.8
  51.3 45.1 all-gather.10
  98.7 36.7 all-gather.12
  149.0 52.9 reduce-scatter.8
  204.3 50.5 all-gather.16
  256.9 31.6 all-gather.14
  290.2 33.1 all-gather.20
  325.7 50.5 all-gather.18
  398.2 52.7 reduce-scatter.12
  453.2 54.2 reduce-scatter.10
  515.1 33.1 all-gather.22
  552.4 72.4 reduce-scatter.22
  628.8 71.3 reduce-scatter.20
  704.1 56.6 reduce-scatter.18
  764.4 65.3 reduce-scatter.16
  831.9 53.1 reduce-scatter.14
where the time goes:
time: 947 us; the launch traced here: 938 us
  waiting for transfers between devices  509 us (54%)
  matrix products  174 us (18%)
  blocking collectives  103 us (11%)
  other arithmetic  67.7 us (7%)
  local copies, waits for them, and re-layouts  64.5 us (7%)
  between operations  14.6 us (2%)
    reduce_scatter x4, waiting for transfers between devices, rows_sum(): return lax.psum_scatter(term(), 'tensor', scatter_dimension=0, tiled=True)  200 us
    all_gather x4, waiting for transfers between devices, rows_all(): return lax.all_gather(local_rows, 'tensor', axis=0, tiled=True)  105 us
    psum x1, blocking collectives, shards(): qv_bias_total, up_bias_total = lax.psum((qv_bias_grad, up_bias_grad), 'dp')  62.6 us
    reduce_scatter x1, waiting for transfers between devices, shards(): lax.psum_scatter(qkv_weight_grad.astype(jnp.bfloat16), 'dp', scatter_dime...  53.5 us
    all_gather x1, waiting for transfers between devices, shards(): lax.all_gather(down_weight, 'dp', axis=1, tiled=True)  53 us
    all_gather x1, waiting for transfers between devices, shards(): lax.all_gather(qkv_weight, 'dp', axis=0, tiled=True)  47.5 us
    all_gather x1, waiting for transfers between devices, shards(): lax.all_gather(up_weight, 'dp', axis=0, tiled=True)  47.3 us
    dynamic_update_slice x4, local copies, waits for them, and re-layouts, attend_forward(): lax.map(block_attend, (query_blocks, jnp.arange(block_count)))  40.9 us
  transfers between devices with their start and end apart: 16, of which 12 were waited for; matrix products, arithmetic and copies ran while one was open for 27% of the time, Pallas kernels for 0%

commit v1 on v0

v1 whole, which is shorter than its diff:
```python
import jax
import jax.numpy as jnp
from jax import lax
from jax.experimental import pallas as pl
from jax.experimental.pallas import tpu as pltpu
from jax.sharding import PartitionSpec as P

HD = 64
LEN = 1024
QB = 256
SCALE = 0.125
NEG = -1e30
F32 = jnp.float32
BF16 = jnp.bfloat16


eps = 1e-05


def normalize(values_in, gain_vec, shift_vec):
    row_mean = jnp.mean(values_in, axis=-1, keepdims=True)
    centred = values_in - row_mean
    row_var = jnp.mean(centred * centred, axis=-1, keepdims=True)
    return centred * lax.rsqrt(row_var + eps) * gain_vec + shift_vec


def gelu_tanh(hidden):
    return jax.nn.gelu(hidden, approximate=True)


def dot(left, right):
    return jnp.dot(left, right, preferred_element_type=F32)


def contract_rows(left, right):
    return lax.dot_general(left, right, (((0,), (0,)), ((), ())), preferred_element_type=F32)


def contract_cols(left, right):
    return lax.dot_general(left, right, (((1,), (1,)), ((), ())), preferred_element_type=F32)


def probs_columns(query_block, keys, first_row):
    scores = contract_cols(keys, query_block)
    key_ids = lax.broadcasted_iota(jnp.int32, scores.shape, 0)
    row_ids = first_row + lax.broadcasted_iota(jnp.int32, scores.shape, 1)
    scores = jnp.where(key_ids <= row_ids, scores, NEG)
    exp_scores = jnp.exp(scores - jnp.max(scores, axis=0, keepdims=True))
    return exp_scores * (1.0 / jnp.sum(exp_scores, axis=0, keepdims=True))


def forward_kernel(qkv_ref, out_ref):
    for head in range(2):
        base = head * 3 * HD
        for block in range(LEN // QB):
            lo, hi = block * QB, (block + 1) * QB
            queries = qkv_ref[lo:hi, base : base + HD] * SCALE
            keys = qkv_ref[:hi, base + HD : base + 2 * HD]
            values = qkv_ref[:hi, base + 2 * HD : base + 3 * HD]
            probs = probs_columns(queries, keys, lo).astype(BF16)
            out_ref[lo:hi, head * HD : (head + 1) * HD] = contract_rows(values, probs).T.astype(BF16)


def backward_kernel(qkv_ref, grad_ref, out_ref, key_acc, value_acc):
    for head in range(2):
        base = head * 3 * HD
        for block in reversed(range(LEN // QB)):
            lo, hi = block * QB, (block + 1) * QB
            queries = qkv_ref[lo:hi, base : base + HD] * SCALE
            keys = qkv_ref[:hi, base + HD : base + 2 * HD]
            values = qkv_ref[:hi, base + 2 * HD : base + 3 * HD]
            grads = grad_ref[lo:hi, head * HD : (head + 1) * HD]
            probs = probs_columns(queries, keys, lo)
            prob_grad = contract_cols(values, grads)
            row_dot = jnp.sum(probs * prob_grad, axis=0, keepdims=True)
            score_grad = (probs * (prob_grad - row_dot)).astype(BF16)
            query_grad = (contract_rows(keys, score_grad) * SCALE).T
            out_ref[lo:hi, base : base + HD] = query_grad.astype(BF16)
            key_part = dot(score_grad, queries)
            value_part = dot(probs.astype(BF16), grads)
            if hi == LEN:
                key_acc[...] = key_part
                value_acc[...] = value_part
            else:
                key_acc[:hi, :] += key_part
                value_acc[:hi, :] += value_part
        out_ref[:, base + HD : base + 2 * HD] = key_acc[...].astype(BF16)
        out_ref[:, base + 2 * HD : base + 3 * HD] = value_acc[...].astype(BF16)


def attention_cost(qkv, products):
    rows, columns = qkv.shape
    pairs = rows * LEN * (columns // (3 * HD))
    return pl.CostEstimate(
        flops=products * pairs * HD * 4, bytes_accessed=4 * rows * columns, transcendentals=pairs
    )


def attend_forward(qkv):
    rows, columns = qkv.shape
    return pl.pallas_call(
        forward_kernel,
        grid=(rows // LEN, columns // (6 * HD)),
        in_specs=[pl.BlockSpec((LEN, 6 * HD), lambda s, h: (s, h))],
        out_specs=pl.BlockSpec((LEN, 2 * HD), lambda s, h: (s, h)),
        out_shape=jax.ShapeDtypeStruct((rows, columns // 3), BF16),
        compiler_params=pltpu.CompilerParams(vmem_limit_bytes=40 * 2**20),
        cost_estimate=attention_cost(qkv, 2),
    )(qkv)


def attend_backward(qkv, heads_grad):
    rows, columns = qkv.shape
    return pl.pallas_call(
        backward_kernel,
        grid=(rows // LEN, columns // (6 * HD)),
        in_specs=[
            pl.BlockSpec((LEN, 6 * HD), lambda s, h: (s, h)),
            pl.BlockSpec((LEN, 2 * HD), lambda s, h: (s, h)),
        ],
        out_specs=pl.BlockSpec((LEN, 6 * HD), lambda s, h: (s, h)),
        out_shape=jax.ShapeDtypeStruct((rows, columns), BF16),
        scratch_shapes=[pltpu.VMEM((LEN, HD), F32), pltpu.VMEM((LEN, HD), F32)],
        compiler_params=pltpu.CompilerParams(vmem_limit_bytes=40 * 2**20),
        cost_estimate=attention_cost(qkv, 5),
    )(qkv, heads_grad)


def swap(values):
    return lax.ppermute(values, "tensor", [(0, 1), (1, 0)])


def total_over(values, axis):
    size = lax.axis_size(axis)
    if size & (size - 1):
        return lax.psum(values, axis)
    step = 1
    while step < size:
        values = values + lax.ppermute(values, axis, [(i, i ^ step) for i in range(size)])
        step *= 2
    return values


class Pair:
    def __init__(self):
        self.first = lax.axis_index("tensor") == 0

    def gather(self, mine):
        return (mine, swap(mine))

    def ordered(self, parts):
        mine, other = parts
        return jnp.where(
            self.first, jnp.concatenate((mine, other)), jnp.concatenate((other, mine))
        )

    def split(self, rows):
        top, low = jnp.split(rows, 2)
        return (jnp.where(self.first, top, low), jnp.where(self.first, low, top))

    def scatter(self, parts, product):
        mine, other = parts
        theirs = swap(product(other).astype(BF16))
        return product(mine) + theirs.astype(F32)


class Group:
    def gather(self, mine):
        return (lax.all_gather(mine, "tensor", axis=0, tiled=True),)

    def ordered(self, parts):
        return parts[0]

    def split(self, rows):
        return (rows,)

    def scatter(self, parts, product):
        summed = lax.psum_scatter(
            product(parts[0]).astype(BF16), "tensor", scatter_dimension=0, tiled=True
        )
        return summed.astype(F32)


def shards(
    inputs,
    qkv_weight,
    qv_bias,
    out_weight,
    out_bias,
    up_weight,
    up_bias,
    down_weight,
    down_bias,
    gain_one,
    shift_one,
    gain_two,
    shift_two,
    cotangent,
):
    group = Pair() if lax.axis_size("tensor") == 2 else Group()
    join = lambda parts: jnp.concatenate(parts) if len(parts) > 1 else parts[0]
    each = lambda fn, parts: tuple(fn(part) for part in parts)
    local_x = inputs.astype(F32)
    head_count = qv_bias.shape[0] // (2 * HD)
    first_norm = normalize(local_x, gain_one, shift_one).astype(BF16)
    first_parts = group.gather(first_norm)
    qkv_full = lax.all_gather(qkv_weight, "dp", axis=0, tiled=True)
    out_full = lax.all_gather(out_weight, "dp", axis=1, tiled=True)
    up_full = lax.all_gather(up_weight, "dp", axis=0, tiled=True)
    down_full = lax.all_gather(down_weight, "dp", axis=1, tiled=True)
    biases = qv_bias.reshape(head_count, 2, HD)
    qkv_bias = jnp.stack(
        (biases[:, 0], jnp.zeros_like(biases[:, 0]), biases[:, 1]), axis=1
    ).reshape(-1)
    qkv = group.ordered(
        each(lambda rows: (dot(rows, qkv_full) + qkv_bias).astype(BF16), first_parts)
    )
    heads_low = attend_forward(qkv)
    heads_parts = group.split(heads_low)
    branch = group.scatter(heads_parts, lambda rows: dot(rows, out_full)) + out_bias
    middle = local_x + branch
    second_norm = normalize(middle, gain_two, shift_two).astype(BF16)
    second_parts = group.gather(second_norm)
    hidden = each(lambda rows: dot(rows, up_full) + up_bias, second_parts)
    active = each(lambda rows: gelu_tanh(rows).astype(BF16), hidden)
    down_out = group.scatter(active, lambda rows: dot(rows, down_full)) + down_bias
    layer_out = (middle + down_out).astype(BF16)

    out_grad = cotangent.astype(F32)
    down_bias_grad = jnp.sum(out_grad, axis=0)
    down_parts = group.gather(cotangent)

    def hidden_back(pair_in):
        rows, grads = pair_in
        active_grad = contract_cols(grads, down_full)
        return jax.vjp(gelu_tanh, rows)[1](active_grad)[0].astype(BF16)

    hidden_parts = each(hidden_back, tuple(zip(hidden, down_parts)))
    second_grad = group.scatter(hidden_parts, lambda rows: contract_cols(rows, up_full))
    down_weight_grad = contract_rows(join(active), join(down_parts)).astype(BF16)
    down_shard = lax.psum_scatter(down_weight_grad, "dp", scatter_dimension=1, tiled=True)
    hidden_low = join(hidden_parts)
    up_bias_grad = jnp.sum(hidden_low, axis=0, dtype=F32)
    up_weight_grad = contract_rows(join(second_parts), hidden_low).astype(BF16)
    up_shard = lax.psum_scatter(up_weight_grad, "dp", scatter_dimension=0, tiled=True)
    norm_pull = jax.vjp(normalize, middle, gain_two, shift_two)[1]
    middle_part, gain_two_grad, shift_two_grad = norm_pull(second_grad)
    middle_grad = out_grad + middle_part
    branch_low = middle_grad.astype(BF16)
    out_bias_grad = jnp.sum(branch_low, axis=0, dtype=F32)
    branch_parts = group.gather(branch_low)
    heads_grad = group.ordered(
        each(lambda rows: contract_cols(rows, out_full).astype(BF16), branch_parts)
    )
    out_weight_grad = contract_rows(join(heads_parts), join(branch_parts)).astype(BF16)
    out_shard = lax.psum_scatter(out_weight_grad, "dp", scatter_dimension=1, tiled=True)
    qkv_low = attend_backward(qkv, heads_grad)
    qkv_parts = group.split(qkv_low)
    qkv_weight_grad = contract_rows(join(first_parts), join(qkv_parts)).astype(BF16)
    qkv_shard = lax.psum_scatter(qkv_weight_grad, "dp", scatter_dimension=0, tiled=True)
    first_grad = group.scatter(qkv_parts, lambda rows: contract_cols(rows, qkv_full))
    bias_sums = jnp.sum(qkv_low, axis=0, dtype=F32).reshape(head_count, 3, HD)
    qv_bias_grad = jnp.stack((bias_sums[:, 0], bias_sums[:, 2]), axis=1).reshape(-1)
    first_pull = jax.vjp(normalize, local_x, gain_one, shift_one)[1]
    input_part, gain_one_grad, shift_one_grad = first_pull(first_grad)
    input_grad = middle_grad + input_part

    width = out_bias.shape[0]
    shared = jnp.concatenate(
        (
            out_bias_grad,
            down_bias_grad,
            gain_two_grad,
            shift_two_grad,
            gain_one_grad,
            shift_one_grad,
        )
    )
    owned = jnp.concatenate((qv_bias_grad, up_bias_grad))
    shared = total_over(shared, "tensor")
    totals = total_over(jnp.concatenate((shared, owned)).reshape(-1, 128), "dp").reshape(-1)
    out_bias_total, down_bias_total, gain_two_total, shift_two_total, gain_one_total, shift_one_total = (
        jnp.split(totals[: 6 * width], 6)
    )
    qv_bias_total, up_bias_total = jnp.split(totals[6 * width :], [qv_bias.shape[0]])
    return (
        layer_out,
        input_grad,
        qkv_shard.astype(F32),
        qv_bias_total,
        out_shard.astype(F32),
        out_bias_total,
        up_shard.astype(F32),
        up_bias_total,
        down_shard.astype(F32),
        down_bias_total,
        gain_one_total,
        shift_one_total,
        gain_two_total,
        shift_two_total,
    )


def solution(mesh):
    in_specs = (
        P(("dp", "tensor"), None),
        P("dp", "tensor"),
        P("tensor"),
        P("tensor", "dp"),
        P(),
        P("dp", "tensor"),
        P("tensor"),
        P("tensor", "dp"),
        P(),
        P(),
        P(),
        P(),
        P(),
        P(("dp", "tensor"), None),
    )
    out_specs = (
        P(("dp", "tensor"), None),
        P(("dp", "tensor"), None),
        P("dp", "tensor"),
        P("tensor"),
        P("tensor", "dp"),
        P(),
        P("dp", "tensor"),
        P("tensor"),
        P("tensor", "dp"),
        P(),
        P(),
        P(),
        P(),
        P(),
    )
    return jax.shard_map(shards, mesh=mesh, in_specs=in_specs, out_specs=out_specs, check_vma=False)
```

time: 947 us -> 599 us (0.63)
  waiting for transfers between devices: 509 us -> 399 us
  blocking collectives: 103 us -> 0 us
  matrix products: 174 us -> 83.1 us
  local copies, waits for them, and re-layouts: 64.5 us -> 8.3 us
  Pallas kernels: 0 us -> 46.7 us
  other arithmetic: 67.7 us -> 24.1 us
  starting transfers between devices: 1.63 us -> 18.8 us
    all_gather x8 -> x4, waiting for transfers between devices: 253 us -> 120 us  [the longest x1 44.6 us: shards(): down_full = lax.all_gather(down_weight, 'dp', axis=1, tiled=True)]
    ppermute x0 -> x13, waiting for transfers between devices: none -> 116 us  [the longest x8 101 us: swap(): return lax.ppermute(values, 'tensor', [(0, 1), (1, 0)])]
    psum x2 -> x0, blocking collectives: 103 us -> none  [the longest x1 62.6 us: shards(): qv_bias_total, up_bias_total = lax.psum((qv_bias_grad, up_bias_grad), 'dp')]
    reduce_scatter x8 -> x4, waiting for transfers between devices: 253 us -> 159 us  [the longest x1 73.4 us: shards(): lax.psum_scatter(up_weight_grad, 'dp', scatter_dimension=0, tiled=True)]
    dot_general x18 -> x8, matrix products: 114 us -> 27.2 us  [dot(): return jnp.dot(left, right, preferred_element_type=F32)]
    pallas_call x0 -> x2, Pallas kernels: none -> 46.7 us  [the longest x1 28.9 us: attend_backward(): pl.pallas_call(backward_kernel, grid=(rows // LEN, columns // (6 * HD)),...]
    dynamic_update_slice x4 -> x0, local copies, waits for them, and re-layouts: 40.9 us -> none  [attend_forward(): lax.map(block_attend, (query_blocks, jnp.arange(block_count)))]
    convert_element_type x10 -> x6, other arithmetic: 34 us -> 7.61 us  [the longest x1 1.78 us: shards(): up_shard.astype(F32)]
  transfers between devices with their start and end apart: 16 -> 21, of which waited for: 12 -> 17; matrix products, arithmetic and copies ran while one was open for 27% -> 14% of each run, Pallas kernels for 0% -> 8%
where the time goes in v1:
time: 599 us; the launch traced here: 594 us
  waiting for transfers between devices  399 us (67%)
  matrix products  83.1 us (14%)
  Pallas kernels  46.7 us (8%)
  other arithmetic  24.1 us (4%)
  starting transfers between devices  18.8 us (3%)
  between operations  14.9 us (2%)
  local copies, waits for them, and re-layouts  8.3 us (1%)
    ppermute x8, waiting for transfers between devices, swap(): return lax.ppermute(values, 'tensor', [(0, 1), (1, 0)])  101 us
    reduce_scatter x1, waiting for transfers between devices, shards(): lax.psum_scatter(up_weight_grad, 'dp', scatter_dimension=0, tiled=True)  73.4 us
    reduce_scatter x1, waiting for transfers between devices, shards(): lax.psum_scatter(qkv_weight_grad, 'dp', scatter_dimension=0, tiled=True)  67.9 us
    all_gather x1, waiting for transfers between devices, shards(): down_full = lax.all_gather(down_weight, 'dp', axis=1, tiled=True)  44.6 us
    all_gather x1, waiting for transfers between devices, shards(): qkv_full = lax.all_gather(qkv_weight, 'dp', axis=0, tiled=True)  42.7 us
    dot_general x8, matrix products, contract_cols(): lax.dot_general(left, right, (((1,), (1,)), ((), ())), preferred_element_...  30.8 us
    pallas_call x1, Pallas kernels, attend_backward(): pl.pallas_call(backward_kernel, grid=(rows // LEN, columns // (6 * HD)),...  28.9 us
    dot_general x8, matrix products, dot(): return jnp.dot(left, right, preferred_element_type=F32)  27.2 us
  transfers between devices with their start and end apart: 21, of which 17 were waited for; matrix products, arithmetic and copies ran while one was open for 14% of the time, Pallas kernels for 8%

profile of v1, /device:TPU:0, one launch (start us, length us, event | category | flops | bytes accessed | tf_op | source)
XLA Modules:
  0.0 594.5 jit_solution(684631935731645)
XLA Ops:
  12.4 3.0 collective-permute-start
  15.8 42.7 %all-gather.5.cloned.1.call-done = bf16[1024,1536]{1,0:T(8,128)(2,1)} async-done(((bf16[64,1536]{1,0:T(8,128)(2,1)}), bf16[1024,1536]{1,0:T(8,128)(2,1)}) %all-gather.5.cloned.1.call-update) | async-done | bytes 3145744 | tf_op jit(solution)/shard_map/all_gather | solution.py:207
  58.5 3.8 fusion.28
  65.7 17.8 %shard_map.245 = bf16[1024,512]{1,0:T(8,128)(2,1)S(1)} custom-call(bf16[1024,1536]{1,0:T(8,128)(2,1)S(1)} %maximum_select_fusion.qkv_ref), custom_call_target="tpu_custom_call" | custom-call | flops 4294967296 | bytes 6291456 | tf_op jit(solution)/shard_map/pallas_call | solution.py:101
  84.3 13.1 %all-gather.7.cloned.1.call-done = bf16[512,1024]{0,1:T(8,128)(2,1)} async-done(((bf16[512,64]{0,1:T(8,128)(2,1)}), bf16[512,1024]{0,1:T(8,128)(2,1)}) %all-gather.7.cloned.1.call-update) | async-done | bytes 1048592 | tf_op jit(solution)/shard_map/all_gather | solution.py:208
  101.7 24.0 %collective-permute-done.1 = bf16[512,1024]{1,0:T(8,128)(2,1)S(1)} collective-permute-done((bf16[512,1024]{1,0:T(8,128)(2,1)S(1)}, bf16[512,1024]{1,0:T(8,128)(2,1)S(1)}, u32[]{:S(2)}, u32[]{:S(2)}) %collective-permute-start.1) | collective-permute-done | bytes 1048608 | tf_op jit(solution)/shard_map/ppermute | solution.py:130
  129.3 19.9 %all-gather.9.cloned.1.call-done = bf16[1024,2048]{1,0:T(8,128)(2,1)} async-done(((bf16[64,2048]{1,0:T(8,128)(2,1)}), bf16[1024,2048]{1,0:T(8,128)(2,1)}) %all-gather.9.cloned.1.call-update) | async-done | bytes 4194320 | tf_op jit(solution)/shard_map/all_gather | solution.py:209
  149.1 6.5 %fusion.72 = f32[512,2048]{1,0:T(8,128)} fusion(bf16[512,1024]{1,0:T(8,128)(2,1)S(1)} %add_convert_fusion.1, bf16[1024,2048]{1,0:T(8,128)(2,1)} %all-gather.9.cloned.1.call-done), kind=kOutput, calls=%fused_computation.133 | convolution fusion | flops 2147483648 | bytes 9437184 | tf_op jit(solution)/shard_map/dot_general | solution.py:32
  155.6 44.6 %all-gather.11.cloned.1.call-done = bf16[2048,1024]{0,1:T(8,128)(2,1)} async-done(((bf16[2048,64]{0,1:T(8,128)(2,1)}), bf16[2048,1024]{0,1:T(8,128)(2,1)}) %all-gather.11.cloned.1.call-update) | async-done | bytes 4194320 | tf_op jit(solution)/shard_map/all_gather | solution.py:210
  200.2 5.0 fusion.74
  205.3 5.8 fusion.73
  211.1 10.9 %fusion.13 = (bf16[512,2048]{1,0:T(8,128)(2,1)S(1)}, bf16[512,2048]{1,0:T(8,128)(2,1)S(1)}, bf16[512,2048]{1,0:T(8,128)(2,1)}, bf16[512,2048]{1,0:T(8,128)(2,1)S(1)}) fusion(f32[512,2048]{1,0:T(8,128)} %fusion.73, f32[2048]{0:T(1024)S(1)} %copy-done.32, f32[512,2048]{1,0:T(8,128)S(1)} %copy-done.35, f32[512,2048]{1,0:T(8,128)S(1)} %fusion.74, ...), kind=kOutput, calls=%fused_computation.19 | convolution fusion | flops 2195718144 | bytes 26222592 | tf_op jit(solution)/shard_map/dot_general | solution.py:40
  228.9 21.5 %collective-permute-done.5 = bf16[512,1024]{1,0:T(8,128)(2,1)S(1)} collective-permute-done((bf16[512,1024]{1,0:T(8,128)(2,1)S(1)}, bf16[512,1024]{1,0:T(8,128)(2,1)S(1)}, u32[]{:S(2)}, u32[]{:S(2)}) %collective-permute-start.5) | collective-permute-done | bytes 1048608 | tf_op jit(solution)/shard_map/ppermute | solution.py:130
  250.5 3.0 multiply_reduce_fusion
  253.5 18.8 %collective-permute-done.3 = bf16[512,1024]{1,0:T(8,128)(2,1)S(1)} collective-permute-done((bf16[512,1024]{1,0:T(8,128)(2,1)S(1)}, bf16[512,1024]{1,0:T(8,128)(2,1)S(1)}, u32[]{:S(2)}, u32[]{:S(2)}) %collective-permute-start.3) | collective-permute-done | bytes 1048608 | tf_op jit(solution)/shard_map/ppermute | solution.py:130
  272.3 3.9 fusion.68
  280.1 23.0 %collective-permute-done.6 = bf16[512,1024]{1,0:T(8,128)(2,1)S(1)} collective-permute-done((bf16[512,1024]{1,0:T(8,128)(2,1)S(1)}, bf16[512,1024]{1,0:T(8,128)(2,1)S(1)}, u32[]{:S(2)}, u32[]{:S(2)}) %collective-permute-start.6) | collective-permute-done | bytes 1048608 | tf_op jit(solution)/shard_map/ppermute | solution.py:130
  306.7 8.7 %fusion.18 = bf16[2048,1024]{0,1:T(8,128)(2,1)} fusion(bf16[512,2048]{1,0:T(8,128)(2,1)S(1)} %copy-done.37, bf16[512,2048]{1,0:T(8,128)(2,1)} %get-tuple-element.48, bf16[512,1024]{1,0:T(8,128)(2,1)} %collective-permute-done.4, bf16[512,1024]{1,0:T(8,128)(2,1)} %param.27), kind=kOutput, calls=%fused_computation.27 | convolution fusion | flops 4309647360 | bytes 10485760 | tf_op jit(solution)/shard_map/dot_general | solution.py:36
  317.0 8.9 %convolution_convert_fusion.1 = bf16[1024,2048]{1,0:T(8,128)(2,1)} fusion(bf16[512,2048]{1,0:T(8,128)(2,1)S(1)} %copy-done.7, bf16[512,2048]{1,0:T(8,128)(2,1)} %copy-done.8, bf16[512,1024]{1,0:T(8,128)(2,1)} %collective-permute-done.2, bf16[512,1024]{1,0:T(8,128)(2,1)} %copy-done.12), kind=kOutput, calls=%fused_computation.29 | convolution fusion | flops 4309647360 | bytes 10485760 | tf_op jit(solution)/shard_map/dot_general | solution.py:36
  329.8 28.9 %shard_map.246 = bf16[1024,1536]{1,0:T(8,128)(2,1)S(1)} custom-call(bf16[1024,1536]{1,0:T(8,128)(2,1)S(1)} %copy-done.1, bf16[1024,512]{1,0:T(8,128)(2,1)S(1)} %maximum_select_fusion.1.grad_ref), custom_call_target="tpu_custom_call" | custom-call | flops 10737418240 | bytes 6291456 | tf_op jit(solution)/shard_map/pallas_call | solution.py:114
  361.1 2.9 convolution_convert_fusion.2
  365.5 5.3 convolution_convert_fusion
  370.8 2.9 convert_reduce_fusion
  374.4 13.6 %collective-permute-done.7 = bf16[512,1024]{1,0:T(8,128)(2,1)} collective-permute-done((bf16[512,1024]{1,0:T(8,128)(2,1)}, bf16[512,1024]{1,0:T(8,128)(2,1)}, u32[]{:S(2)}, u32[]{:S(2)}) %collective-permute-start.7) | collective-permute-done | bytes 1048608 | tf_op jit(solution)/shard_map/ppermute | solution.py:130
  388.0 5.2 fusion.34
  395.5 3.1 convert_reduce_fusion.3
  404.4 4.2 collective-permute-done.10
  410.3 2.8 collective-permute-done.11
  415.1 4.9 collective-permute-done.12
  422.8 18.1 %reduce-scatter.11.cloned.1.call-done = bf16[2048,64]{0,1:T(8,128)(2,1)} async-done(((bf16[2048,1024]{0,1:T(8,128)(2,1)}), bf16[2048,64]{0,1:T(8,128)(2,1)}) %reduce-scatter.11.cloned.1.call-update) | async-done | bytes 262160 | tf_op jit(solution)/shard_map/reduce_scatter | solution.py:241
  442.6 73.4 %reduce-scatter.9.cloned.1.call-done = bf16[64,2048]{1,0:T(8,128)(2,1)} async-done(((bf16[1024,2048]{1,0:T(8,128)(2,1)}), bf16[64,2048]{1,0:T(8,128)(2,1)}) %reduce-scatter.9.cloned.1.call-update) | async-done | bytes 262160 | tf_op jit(solution)/shard_map/reduce_scatter | solution.py:245
  517.9 67.9 %reduce-scatter.5.cloned.1.call-done = bf16[64,1536]{1,0:T(8,128)(2,1)} async-done(((bf16[1024,1536]{1,0:T(8,128)(2,1)}), bf16[64,1536]{1,0:T(8,128)(2,1)}) %reduce-scatter.5.cloned.1.call-update) | async-done | bytes 196624 | tf_op jit(solution)/shard_map/reduce_scatter | solution.py:260
  (167 shorter events, 61.5 us)
Async XLA Ops:
  7.2 51.3 %all-gather.5.cloned.1.call-start = ((), (), s32[]{:S(2)}) async-start(), calls=%async_computation.4 | async-start | bytes 3342336 | tf_op jit(solution)/shard_map/all_gather | solution.py:207
  7.9 89.5 %all-gather.7.cloned.1.call-start = ((), (), s32[]{:S(2)}) async-start(), calls=%async_computation.5 | async-start | bytes 1114112 | tf_op jit(solution)/shard_map/all_gather | solution.py:208
  8.7 140.4 %all-gather.9.cloned.1.call-start = ((), (), s32[]{:S(2)}) async-start(), calls=%async_computation.6 | async-start | bytes 4456448 | tf_op jit(solution)/shard_map/all_gather | solution.py:209
  9.4 190.8 %all-gather.11.cloned.1.call-start = ((), (), s32[]{:S(2)}) async-start(), calls=%async_computation.7 | async-start | bytes 4456448 | tf_op jit(solution)/shard_map/all_gather | solution.py:210
  10.0 411.2 %reduce-scatter.7.cloned.1.call-start = ((), (), s32[]{:S(2)}) async-start(), calls=%async_computation.9 | async-start | bytes 1114112 | tf_op jit(solution)/shard_map/reduce_scatter | solution.py:256
  12.4 49.9 %copy-start.10 = (bf16[512,1024]{1,0:T(8,128)(2,1)}, bf16[512,1024]{1,0:T(8,128)(2,1)S(1)}, u32[]{:S(2)}) copy-start(bf16[512,1024]{1,0:T(8,128)(2,1)S(1)} %fusion.33) | copy-start | bytes 3145732
  12.4 49.9 %collective-permute-start = (bf16[512,1024]{1,0:T(8,128)(2,1)S(1)}, bf16[512,1024]{1,0:T(8,128)(2,1)S(1)}, u32[]{:S(2)}, u32[]{:S(2)}) collective-permute-start(bf16[512,1024]{1,0:T(8,128)(2,1)S(1)} %fusion.33), channel_id=1, source_target_pairs={{0,1},{1,0},{2,3},{3,2},{4,5},{5,4},{6,7},{7,6},{8,9},{9,8},{10,11... | collective-permute-start | bytes 3145736 | tf_op jit(solution)/shard_map/ppermute | solution.py:130
  83.5 42.2 %copy-start.33 = (f32[1024]{0:T(1024)S(1)}, f32[1024]{0:T(1024)}, u32[]{:S(2)}) copy-start(f32[1024]{0:T(1024)} %param.18) | copy-start | bytes 12292
  84.3 41.3 %copy-start.13 = (bf16[512,512]{1,0:T(8,128)(2,1)}, bf16[512,512]{1,0:T(8,128)(2,1)S(1)}, u32[]{:S(2)}) copy-start(bf16[512,512]{1,0:T(8,128)(2,1)S(1)} %get-tuple-element.37) | copy-start | bytes 1572868
  97.5 28.2 %copy-start.15 = (bf16[512,512]{1,0:T(8,128)(2,1)S(1)}, bf16[512,512]{1,0:T(8,128)(2,1)}, u32[]{:S(2)}) copy-start(bf16[512,512]{1,0:T(8,128)(2,1)} %get-tuple-element.38) | copy-start | bytes 1572868
  97.5 28.2 %copy-start.26 = (bf16[512,1024]{0,1:T(8,128)(2,1)S(1)}, bf16[512,1024]{0,1:T(8,128)(2,1)}, u32[]{:S(2)}) copy-start(bf16[512,1024]{0,1:T(8,128)(2,1)} %all-gather.7.cloned.1.call-done) | copy-start | bytes 3145732
  99.6 26.1 %collective-permute-start.1 = (bf16[512,1024]{1,0:T(8,128)(2,1)S(1)}, bf16[512,1024]{1,0:T(8,128)(2,1)S(1)}, u32[]{:S(2)}, u32[]{:S(2)}) collective-permute-start(bf16[512,1024]{1,0:T(8,128)(2,1)S(1)} %convolution_convert_fusion.3), channel_id=1, source_target_pairs={{0,1},{1,0},{2,3},{3,2},{4,5},{5,4},{6,7},{7,6},{8,9},{9,8},{10,11... | collective-permute-start | bytes 3145736 | tf_op jit(solution)/shard_map/ppermute | solution.py:130
  101.1 110.0 %collective-permute-start.4 = (bf16[512,1024]{1,0:T(8,128)(2,1)}, bf16[512,1024]{1,0:T(8,128)(2,1)}, u32[]{:S(2)}, u32[]{:S(2)}) collective-permute-start(bf16[512,1024]{1,0:T(8,128)(2,1)} %param.27), channel_id=1, source_target_pairs={{0,1},{1,0},{2,3},{3,2},{4,5},{5,4},{6,7},{7,6},{8,9},{9,8},{10,11... | collective-permute-start | bytes 3145736 | tf_op jit(solution)/shard_map/ppermute | solution.py:130
  127.7 27.9 %copy-start.12 = (bf16[512,1024]{1,0:T(8,128)(2,1)}, bf16[512,1024]{1,0:T(8,128)(2,1)S(1)}, u32[]{:S(2)}) copy-start(bf16[512,1024]{1,0:T(8,128)(2,1)S(1)} %add_convert_fusion.1) | copy-start | bytes 3145732
  127.7 77.5 %collective-permute-start.2 = (bf16[512,1024]{1,0:T(8,128)(2,1)S(1)}, bf16[512,1024]{1,0:T(8,128)(2,1)}, u32[]{:S(2)}, u32[]{:S(2)}) collective-permute-start(bf16[512,1024]{1,0:T(8,128)(2,1)S(1)} %add_convert_fusion.1), channel_id=1, source_target_pairs={{0,1},{1,0},{2,3},{3,2},{4,5},{5,4},{6,7},{7,6},{8,9},{9,8},{10,11... | collective-permute-start | bytes 3145736 | tf_op jit(solution)/shard_map/ppermute | solution.py:130
  222.0 28.4 %copy-start.8 = (bf16[512,2048]{1,0:T(8,128)(2,1)}, bf16[512,2048]{1,0:T(8,128)(2,1)S(1)}, u32[]{:S(2)}) copy-start(bf16[512,2048]{1,0:T(8,128)(2,1)S(1)} %get-tuple-element.49) | copy-start | bytes 6291460
  224.4 26.1 %collective-permute-start.5 = (bf16[512,1024]{1,0:T(8,128)(2,1)S(1)}, bf16[512,1024]{1,0:T(8,128)(2,1)S(1)}, u32[]{:S(2)}, u32[]{:S(2)}) collective-permute-start(bf16[512,1024]{1,0:T(8,128)(2,1)S(1)} %convolution_convert_fusion.4), channel_id=1, source_target_pairs={{0,1},{1,0},{2,3},{3,2},{4,5},{5,4},{6,7},{7,6},{8,9},{9,8},{10,11... | collective-permute-start | bytes 3145736 | tf_op jit(solution)/shard_map/ppermute | solution.py:130
  228.3 43.9 %collective-permute-start.3 = (bf16[512,1024]{1,0:T(8,128)(2,1)S(1)}, bf16[512,1024]{1,0:T(8,128)(2,1)S(1)}, u32[]{:S(2)}, u32[]{:S(2)}) collective-permute-start(bf16[512,1024]{1,0:T(8,128)(2,1)S(1)} %convolution_convert_fusion.5), channel_id=1, source_target_pairs={{0,1},{1,0},{2,3},{3,2},{4,5},{5,4},{6,7},{7,6},{8,9},{9,8},{10,11... | collective-permute-start | bytes 3145736 | tf_op jit(solution)/shard_map/ppermute | solution.py:130
  250.5 21.8 %copy-start.38 = (bf16[512,2048]{1,0:T(8,128)(2,1)S(1)}, bf16[512,2048]{1,0:T(8,128)(2,1)}, u32[]{:S(2)}) copy-start(bf16[512,2048]{1,0:T(8,128)(2,1)} %get-tuple-element.48) | copy-start | bytes 6291460
  276.1 28.0 %copy-start.14 = (bf16[512,512]{1,0:T(8,128)(2,1)S(1)}, bf16[512,512]{1,0:T(8,128)(2,1)}, u32[]{:S(2)}) copy-start(bf16[512,512]{1,0:T(8,128)(2,1)} %copy-done.13) | copy-start | bytes 1572868
  276.1 28.0 %copy-start.16 = (bf16[512,512]{1,0:T(8,128)(2,1)S(1)}, bf16[512,512]{1,0:T(8,128)(2,1)}, u32[]{:S(2)}) copy-start(bf16[512,512]{1,0:T(8,128)(2,1)} %get-tuple-element.38) | copy-start | bytes 1572868
  278.6 28.2 %copy-start.37 = (bf16[512,2048]{1,0:T(8,128)(2,1)S(1)}, bf16[512,2048]{1,0:T(8,128)(2,1)}, u32[]{:S(2)}) copy-start(bf16[512,2048]{1,0:T(8,128)(2,1)} %copy-done.36) | copy-start | bytes 6291460
  278.6 24.6 %collective-permute-start.6 = (bf16[512,1024]{1,0:T(8,128)(2,1)S(1)}, bf16[512,1024]{1,0:T(8,128)(2,1)S(1)}, u32[]{:S(2)}, u32[]{:S(2)}) collective-permute-start(bf16[512,1024]{1,0:T(8,128)(2,1)S(1)} %get-tuple-element.21), channel_id=1, source_target_pairs={{0,1},{1,0},{2,3},{3,2},{4,5},{5,4},{6,7},{7,6},{8,9},{9,8},{10,11... | collective-permute-start | bytes 3145736 | tf_op jit(solution)/shard_map/ppermute | solution.py:130
  306.5 134.4 %reduce-scatter.11.cloned.1.call-start = ((), (), s32[]{:S(2)}) async-start(), calls=%async_computation.11 | async-start | bytes 4456448 | tf_op jit(solution)/shard_map/reduce_scatter | solution.py:241
  315.4 200.6 %reduce-scatter.9.cloned.1.call-start = ((), (), s32[]{:S(2)}) async-start(), calls=%async_computation.10 | async-start | bytes 4456448 | tf_op jit(solution)/shard_map/reduce_scatter | solution.py:245
  326.0 259.8 %reduce-scatter.5.cloned.1.call-start = ((), (), s32[]{:S(2)}) async-start(), calls=%async_computation.8 | async-start | bytes 3342336 | tf_op jit(solution)/shard_map/reduce_scatter | solution.py:260
  364.1 23.9 %collective-permute-start.7 = (bf16[512,1024]{1,0:T(8,128)(2,1)}, bf16[512,1024]{1,0:T(8,128)(2,1)}, u32[]{:S(2)}, u32[]{:S(2)}) collective-permute-start(bf16[512,1024]{1,0:T(8,128)(2,1)} %convolution_convert_fusion.2), channel_id=1, source_target_pairs={{0,1},{1,0},{2,3},{3,2},{4,5},{5,4},{6,7},{7,6},{8,9},{9,8},{10,11... | collective-permute-start | bytes 3145736 | tf_op jit(solution)/shard_map/ppermute | solution.py:130
  398.6 3.9 collective-permute-start.8
  402.5 1.3 collective-permute-start.9
  403.8 4.8 collective-permute-start.10
  408.6 4.4 collective-permute-start.11
  413.0 7.0 %collective-permute-start.12 = (f32[72,128]{1,0:T(8,128)S(1)}, f32[72,128]{1,0:T(8,128)S(1)}, u32[]{:S(2)}, u32[]{:S(2)}) collective-permute-start(f32[72,128]{1,0:T(8,128)S(1)} %add.181), channel_id=1, source_target_pairs={{0,16},{2,18},{4,20},{6,22},{8,24},{10,26},{12,28},{14,30},{16,0},... | collective-permute-start | bytes 110600 | tf_op jit(solution)/shard_map/ppermute | solution.py:139
  (28 other events, 144.0 us)
Sparse Core Ops, SparseCore 0:
  10.3 48.0 all-gather.4
  60.6 36.7 all-gather.6
  99.6 49.4 all-gather.8
  151.2 49.0 all-gather.10
  306.6 55.9 reduce-scatter.6
  366.8 74.0 reduce-scatter.10
  444.7 71.3 reduce-scatter.8
  520.4 65.3 reduce-scatter.4
